TPU v7x, 512 devices: a whole 4x4x16 slice. The times are simulated.
512 devices in a mesh: freq: 16 (over y, x), patch: 32 (over z, core).
Axes of the slice: x: 4, y: 4, z: 16, core: 2. Of those that a mesh axis runs over, the one named last changes fastest.
Arguments:
- responses: bfloat16 [2048, 2, 2048], P('patch', None, 'freq'), may hold values from -6 to 6
- adjoints: bfloat16 [2048, 2, 2048], P('patch', None, 'freq'), may hold values from -6 to 6
- patch_shapes: bfloat16 [3072, 4, 48, 128], P('patch'), may hold values from -0.25 to 0.25
- block_lists: int32 [3072, 4], P('patch'), may hold values from 0 to 15
- block_counts: int32 [3072], P('patch'), may hold values from 1 to 4
- patch_sizes: int32 [3072], P('patch'), may hold values from 12 to 48
- owner_map: int32 [3072], P('patch'), may hold values from 0 to 3071, each once
Outputs:
- loss_gradient: float32 [3072], P('patch')
Inputs may be any that keep to these rules, and one draw needn't show every extreme that they name: `owner_map`: each patch appears once.
All inputs are finite; a program needn't handle non-finite values.
Results may differ from a plain program's by a relative error of at most 0.0003.
Values may be sent and summed in bfloat16 or wider, within the bound.
A program may use at most 64 MiB of HBM per device.

v0:
```python
import math

import jax
import jax.numpy as jnp
from jax import lax
from jax.sharding import PartitionSpec as P


def strain_terms(total, masked, blocks, resp_piece, adjo_piece, width):
    count = resp_piece.shape[0]
    modes = resp_piece.shape[2]
    patches = masked.shape[0]
    samples = masked.shape[2]
    step = math.gcd(count, 32)
    turns = count // step

    def one(index, carry):
        resp = lax.dynamic_slice_in_dim(resp_piece, index * step, step, 0).reshape(
            step * 2, modes // width, width
        )
        adjo = lax.dynamic_slice_in_dim(adjo_piece, index * step, step, 0).reshape(
            step * 2, modes // width, width
        )
        forward = jnp.einsum(
            "pksb,cpkb->cps", masked, resp[:, blocks, :], preferred_element_type=jnp.float32
        )
        backward = jnp.einsum(
            "pksb,cpkb->cps", masked, adjo[:, blocks, :], preferred_element_type=jnp.float32
        )
        forward = forward.reshape(step, 2, patches, samples)
        backward = backward.reshape(step, 2, patches, samples)
        cross = forward[:, 0] * backward[:, 1] - forward[:, 1] * backward[:, 0]
        return carry + jnp.sum(cross, axis=(0, 2))

    return lax.fori_loop(0, turns, one, total)


def body(responses, adjoints, patch_shapes, block_lists, block_counts, patch_sizes, owner_map):
    patch_dev, slots, samples, width = patch_shapes.shape
    slot_live = jnp.arange(slots, dtype=jnp.int32)[None, :] < block_counts[:, None]
    row_live = jnp.arange(samples, dtype=jnp.int32)[None, :] < patch_sizes[:, None]
    live = (slot_live[:, :, None, None] & row_live[:, None, :, None]).astype(jnp.bfloat16)
    masked = patch_shapes * live
    freqs = responses.shape[0] * lax.axis_size("patch")
    empty = jnp.zeros((patch_dev,), jnp.float32)
    regrouped = (
        lax.all_to_all(responses, "freq", split_axis=0, concat_axis=2, tiled=True),
        lax.all_to_all(adjoints, "freq", split_axis=0, concat_axis=2, tiled=True),
    )
    terms = strain_terms(
        empty,
        masked,
        block_lists,
        lax.all_gather(regrouped[0], "patch", axis=0, tiled=True),
        lax.all_gather(regrouped[1], "patch", axis=0, tiled=True),
        width,
    )
    terms = terms * (samples * freqs) ** (-0.5)
    patches = patch_dev * lax.axis_size("patch")
    columns = jnp.arange(patches, dtype=jnp.int32)
    onehot = (owner_map[:, None] == columns[None, :]).astype(jnp.float32)
    dense = jnp.dot(terms, onehot, precision=lax.Precision.HIGHEST)
    mine = lax.psum_scatter(dense, "patch", scatter_dimension=0, tiled=True)
    return lax.psum(mine, "freq")


def solution(mesh):
    placed = (
        P("patch", None, "freq"),
        P("patch", None, "freq"),
        P("patch", None, None, None),
        P("patch", None),
        P("patch"),
        P("patch"),
        P("patch"),
    )
    return jax.shard_map(body, mesh=mesh, in_specs=placed, out_specs=P("patch"), check_vma=False)
```

profile of v0, /device:TPU:1, one launch (start us, length us, event | category | flops | bytes accessed | tf_op | source)
XLA Modules:
  0.0 480.2 jit_solution(6683167722934066681)
XLA Ops:
  6.5 14.0 %all_to_all.36 = bf16[64,2,128]{2,1,0:T(2,128)(2,1)S(1)} all-to-all(bf16[64,2,128]{2,1,0:T(2,128)(2,1)} %param.9), channel_id=1, replica_groups=mesh['freq'=16,'patch'=32] {'freq'}, dimensions={0} | all-to-all | bytes 65536 | tf_op jit(solution)/shard_map/all_to_all | solution.py:47
  21.3 9.9 %all_to_all.37 = bf16[64,2,128]{2,1,0:T(2,128)(2,1)S(1)} all-to-all(bf16[64,2,128]{2,1,0:T(2,128)(2,1)} %param.10), channel_id=1, replica_groups=mesh['freq'=16,'patch'=32] {'freq'}, dimensions={0} | all-to-all | bytes 65536 | tf_op jit(solution)/shard_map/all_to_all | solution.py:48
  36.2 6.3 %broadcast_multiply_fusion = bf16[96,4,48,128]{3,2,1,0:T(8,128)(2,1)} fusion(bf16[96,4,48,128]{3,2,1,0:T(8,128)(2,1)} %param.11, bf16[96,4,48]{2,1,0:T(4,128)(2,1)S(1)} %and_convert_fusion), kind=kLoop, calls=%fused_computation.14 | loop fusion | flops 2359296 | bytes 9474048 | tf_op jit(solution)/shard_map/mul | solution.py:43
  42.5 52.1 %all-gather.3.cloned.1.call-done = bf16[128,2,2048]{2,1,0:T(2,128)(2,1)} async-done(((bf16[4,2,2048]{2,1,0:T(2,128)(2,1)}), bf16[128,2,2048]{2,1,0:T(2,128)(2,1)}) %all-gather.3.cloned.1.call-update) | async-done | bytes 1048592 | tf_op jit(solution)/shard_map/all_gather | solution.py:54
  94.6 70.0 %all-gather.5.cloned.1.call-done = bf16[128,2,2048]{2,1,0:T(2,128)(2,1)} async-done(((bf16[4,2,2048]{2,1,0:T(2,128)(2,1)}), bf16[128,2,2048]{2,1,0:T(2,128)(2,1)}) %all-gather.5.cloned.1.call-update) | async-done | bytes 1048592 | tf_op jit(solution)/shard_map/all_gather | solution.py:55
  164.6 185.4 %while.14 = (s32[]{:T(128)}, f32[96]{0:T(128)S(1)}, bf16[128,2,2048]{2,1,0:T(2,128)(2,1)}, s32[96,4]{1,0:T(8,128)S(1)}, bf16[96,4,48,128]{3,2,1,0:T(8,128)(2,1)}...) while((s32[]{:T(128)}, f32[96]{0:T(128)S(1)}, ...), condition=%wide.region_2.0_spmd.clone, body=%wide.region_0.0_spmd.clone.sunk | while | flops 604571840 | bytes 59785376 | solution.py:35
  166.4 13.3 %gather_fusion = bf16[384,64,128]{2,1,0:T(8,128)(2,1)} fusion(bf16[64,16,128]{2,0,1:T(8,128)(2,1)S(1)} %copy.39, s32[1024]{0:T(1024)S(1)} %pad_clamp_fusion.2), kind=kCustom, calls=%fused_computation.1.clone.clone.1 | custom fusion | bytes 12584448 | tf_op jit(solution)/shard_map/while/body/eval_jaxpr/gather | solution.py:28
  179.7 5.9 %convolution_bitcast_fusion.4 = f32[64,96,48]{0,2,1:T(8,128)S(1)} fusion(bf16[64,96,4,128]{3,0,2,1:T(8,128)(2,1)} %bitcast.66, bf16[96,4,48,128]{3,2,1,0:T(8,128)(2,1)} %get-tuple-element.233), kind=kOutput, calls=%fused_computation.2.clone.1 | convolution fusion | flops 301989888 | bytes 12189696 | tf_op jit(solution)/shard_map/while/body/eval_jaxpr/pksb,cpkb->cps/dot_general | solution.py:27
  187.7 13.3 %gather_fusion.1 = bf16[384,64,128]{2,1,0:T(8,128)(2,1)} fusion(bf16[64,16,128]{2,0,1:T(8,128)(2,1)S(1)} %copy.41, s32[1024]{0:T(1024)S(1)} %pad_clamp_fusion.2), kind=kCustom, calls=%fused_computation.clone.clone.1 | custom fusion | bytes 12584448 | tf_op jit(solution)/shard_map/while/body/eval_jaxpr/gather | solution.py:25
  201.0 5.9 %convolution_bitcast_fusion.5 = f32[64,96,48]{0,2,1:T(8,128)S(1)} fusion(bf16[64,96,4,128]{3,0,2,1:T(8,128)(2,1)} %bitcast.65, bf16[96,4,48,128]{3,2,1,0:T(8,128)(2,1)} %get-tuple-element.233), kind=kOutput, calls=%fused_computation.3.clone.1 | convolution fusion | flops 301989888 | bytes 12189696 | tf_op jit(solution)/shard_map/while/body/eval_jaxpr/pksb,cpkb->cps/dot_general | solution.py:24
  212.7 13.3 %gather_fusion = bf16[384,64,128]{2,1,0:T(8,128)(2,1)} fusion(bf16[64,16,128]{2,0,1:T(8,128)(2,1)S(1)} %copy.39, s32[1024]{0:T(1024)S(1)} %pad_clamp_fusion.2), kind=kCustom, calls=%fused_computation.1.clone.clone.1 | custom fusion | bytes 12584448 | tf_op jit(solution)/shard_map/while/body/eval_jaxpr/gather | solution.py:28
  226.0 5.9 %convolution_bitcast_fusion.4 = f32[64,96,48]{0,2,1:T(8,128)S(1)} fusion(bf16[64,96,4,128]{3,0,2,1:T(8,128)(2,1)} %bitcast.66, bf16[96,4,48,128]{3,2,1,0:T(8,128)(2,1)} %get-tuple-element.233), kind=kOutput, calls=%fused_computation.2.clone.1 | convolution fusion | flops 301989888 | bytes 12189696 | tf_op jit(solution)/shard_map/while/body/eval_jaxpr/pksb,cpkb->cps/dot_general | solution.py:27
  234.1 13.3 %gather_fusion.1 = bf16[384,64,128]{2,1,0:T(8,128)(2,1)} fusion(bf16[64,16,128]{2,0,1:T(8,128)(2,1)S(1)} %copy.41, s32[1024]{0:T(1024)S(1)} %pad_clamp_fusion.2), kind=kCustom, calls=%fused_computation.clone.clone.1 | custom fusion | bytes 12584448 | tf_op jit(solution)/shard_map/while/body/eval_jaxpr/gather | solution.py:25
  247.4 5.9 %convolution_bitcast_fusion.5 = f32[64,96,48]{0,2,1:T(8,128)S(1)} fusion(bf16[64,96,4,128]{3,0,2,1:T(8,128)(2,1)} %bitcast.65, bf16[96,4,48,128]{3,2,1,0:T(8,128)(2,1)} %get-tuple-element.233), kind=kOutput, calls=%fused_computation.3.clone.1 | convolution fusion | flops 301989888 | bytes 12189696 | tf_op jit(solution)/shard_map/while/body/eval_jaxpr/pksb,cpkb->cps/dot_general | solution.py:24
  259.1 13.3 %gather_fusion = bf16[384,64,128]{2,1,0:T(8,128)(2,1)} fusion(bf16[64,16,128]{2,0,1:T(8,128)(2,1)S(1)} %copy.39, s32[1024]{0:T(1024)S(1)} %pad_clamp_fusion.2), kind=kCustom, calls=%fused_computation.1.clone.clone.1 | custom fusion | bytes 12584448 | tf_op jit(solution)/shard_map/while/body/eval_jaxpr/gather | solution.py:28
  272.4 5.9 %convolution_bitcast_fusion.4 = f32[64,96,48]{0,2,1:T(8,128)S(1)} fusion(bf16[64,96,4,128]{3,0,2,1:T(8,128)(2,1)} %bitcast.66, bf16[96,4,48,128]{3,2,1,0:T(8,128)(2,1)} %get-tuple-element.233), kind=kOutput, calls=%fused_computation.2.clone.1 | convolution fusion | flops 301989888 | bytes 12189696 | tf_op jit(solution)/shard_map/while/body/eval_jaxpr/pksb,cpkb->cps/dot_general | solution.py:27
  280.4 13.3 %gather_fusion.1 = bf16[384,64,128]{2,1,0:T(8,128)(2,1)} fusion(bf16[64,16,128]{2,0,1:T(8,128)(2,1)S(1)} %copy.41, s32[1024]{0:T(1024)S(1)} %pad_clamp_fusion.2), kind=kCustom, calls=%fused_computation.clone.clone.1 | custom fusion | bytes 12584448 | tf_op jit(solution)/shard_map/while/body/eval_jaxpr/gather | solution.py:25
  293.8 5.9 %convolution_bitcast_fusion.5 = f32[64,96,48]{0,2,1:T(8,128)S(1)} fusion(bf16[64,96,4,128]{3,0,2,1:T(8,128)(2,1)} %bitcast.65, bf16[96,4,48,128]{3,2,1,0:T(8,128)(2,1)} %get-tuple-element.233), kind=kOutput, calls=%fused_computation.3.clone.1 | convolution fusion | flops 301989888 | bytes 12189696 | tf_op jit(solution)/shard_map/while/body/eval_jaxpr/pksb,cpkb->cps/dot_general | solution.py:24
  305.4 13.3 %gather_fusion = bf16[384,64,128]{2,1,0:T(8,128)(2,1)} fusion(bf16[64,16,128]{2,0,1:T(8,128)(2,1)S(1)} %copy.39, s32[1024]{0:T(1024)S(1)} %pad_clamp_fusion.2), kind=kCustom, calls=%fused_computation.1.clone.clone.1 | custom fusion | bytes 12584448 | tf_op jit(solution)/shard_map/while/body/eval_jaxpr/gather | solution.py:28
  318.8 5.9 %convolution_bitcast_fusion.4 = f32[64,96,48]{0,2,1:T(8,128)S(1)} fusion(bf16[64,96,4,128]{3,0,2,1:T(8,128)(2,1)} %bitcast.66, bf16[96,4,48,128]{3,2,1,0:T(8,128)(2,1)} %get-tuple-element.233), kind=kOutput, calls=%fused_computation.2.clone.1 | convolution fusion | flops 301989888 | bytes 12189696 | tf_op jit(solution)/shard_map/while/body/eval_jaxpr/pksb,cpkb->cps/dot_general | solution.py:27
  326.8 13.3 %gather_fusion.1 = bf16[384,64,128]{2,1,0:T(8,128)(2,1)} fusion(bf16[64,16,128]{2,0,1:T(8,128)(2,1)S(1)} %copy.41, s32[1024]{0:T(1024)S(1)} %pad_clamp_fusion.2), kind=kCustom, calls=%fused_computation.clone.clone.1 | custom fusion | bytes 12584448 | tf_op jit(solution)/shard_map/while/body/eval_jaxpr/gather | solution.py:25
  340.1 5.9 %convolution_bitcast_fusion.5 = f32[64,96,48]{0,2,1:T(8,128)S(1)} fusion(bf16[64,96,4,128]{3,0,2,1:T(8,128)(2,1)} %bitcast.65, bf16[96,4,48,128]{3,2,1,0:T(8,128)(2,1)} %get-tuple-element.233), kind=kOutput, calls=%fused_computation.3.clone.1 | convolution fusion | flops 301989888 | bytes 12189696 | tf_op jit(solution)/shard_map/while/body/eval_jaxpr/pksb,cpkb->cps/dot_general | solution.py:24
  350.5 89.1 %all-reduce = f32[3072]{0:T(1024)S(1)} all-reduce(f32[3072]{0:T(1024)S(1)} %bitcast.73), channel_id=2, replica_groups=mesh['freq'=16,'patch'=32] {'patch'}, use_global_device_ids=true, to_apply=%region_3.0.clone | all-reduce | flops 3072 | bytes 24576
  439.7 33.7 %psum.7 = f32[96]{0:T(128)} all-reduce(f32[96]{0:T(128)S(1)} %dynamic-slice.1), channel_id=1, replica_groups=mesh['freq'=16,'patch'=32] {'freq'}, use_global_device_ids=true, to_apply=%region_4.0 | all-reduce | flops 96 | bytes 768 | tf_op jit(solution)/shard_map/psum | solution.py:64
  (66 shorter events, 36.9 us)
Async XLA Ops:
  6.5 88.1 %all-gather.3.cloned.1.call-start = ((), (), s32[]{:S(2)}) async-start(), calls=%async_computation.2 | async-start | bytes 1081344 | tf_op jit(solution)/shard_map/all_gather | solution.py:54
  21.2 143.3 %all-gather.5.cloned.1.call-start = ((), (), s32[]{:S(2)}) async-start(), calls=%async_computation.3 | async-start | bytes 1081344 | tf_op jit(solution)/shard_map/all_gather | solution.py:55
  164.6 185.4 %copy-start = (s32[96]{0:T(128)S(1)}, s32[96]{0:T(128)}, u32[]{:S(2)}) copy-start(s32[96]{0:T(128)} %param.15) | copy-start | bytes 1156
Sparse Core Ops, SparseCore 0:
  21.4 73.1 all-gather.2
  96.7 67.8 all-gather.4
where the time goes:
time: 487 us; the launch traced here: 480 us
  blocking collectives  147 us (30%)
  local copies, waits for them, and re-layouts  133 us (27%)
  waiting for transfers between devices  122 us (25%)
  matrix products  47.9 us (10%)
  other arithmetic  16.3 us (3%)
  between operations  14.1 us (3%)
    unnamed x1, blocking collectives  89.1 us
    all_gather x1, waiting for transfers between devices, body(): lax.all_gather(regrouped[1], 'patch', axis=0, tiled=True)  70 us
    gather x4, local copies, waits for them, and re-layouts, one(): resp[:, blocks, :]  53.3 us
    gather x4, local copies, waits for them, and re-layouts, one(): adjo[:, blocks, :]  53.3 us
    all_gather x1, waiting for transfers between devices, body(): lax.all_gather(regrouped[0], 'patch', axis=0, tiled=True)  52.1 us
    psum x1, blocking collectives, body(): return lax.psum(mine, 'freq')  33.7 us
    dot_general x4, matrix products, one(): jnp.einsum('pksb,cpkb->cps', masked, adjo[:, blocks, :], preferred_elemen...  23.7 us
    dot_general x4, matrix products, one(): jnp.einsum('pksb,cpkb->cps', masked, resp[:, blocks, :], preferred_elemen...  23.7 us
  transfers between devices with their start and end apart: 2, of which 2 were waited for; matrix products, arithmetic and copies ran while one was open for 2% of the time, Pallas kernels for 0%

commit v1 on v0

v1 whole, which is shorter than its diff:
```python
import functools

import jax
import jax.numpy as jnp
from jax import lax
from jax.experimental import pallas as pl
from jax.experimental.pallas import tpu as pltpu
from jax.sharding import PartitionSpec as P

MESH = pl.DeviceIdType.MESH
F32 = jnp.float32
BF16 = jnp.bfloat16

PLANE = 16
COLUMN = 32
RING = 16
HOPS = 8
PATCHES = 96
SLOTS = 4
SAMPLES = 48
WIDTH = 128
PIECE = 16
QUARTERS = 4
UNROLL = 8


def from_left(hop):
    return 2 * hop - 1


def from_right(hop):
    return 2 * hop


def kernel(
    scale,
    resp_ref,
    adjo_ref,
    lists_ref,
    counts_ref,
    sizes_ref,
    owner_ref,
    shapes_hbm,
    out_ref,
    staged,
    x0,
    x1,
    x2,
    x3,
    shapes,
    acc,
    folded,
    dense,
    got_column,
    row,
    got_plane,
    shapes_sem,
    mix_send,
    mix_recv,
    right_send,
    left_send,
    right_recv,
    left_recv,
    pair_send,
    pair_recv,
    column_send,
    column_recv,
    plane_send,
    plane_recv,
):
    quarters = (x0, x1, x2, x3)
    q = lax.axis_index("freq")
    p = lax.axis_index("patch")
    right = (q, lax.rem(p + 2, COLUMN))
    left = (q, lax.rem(p + COLUMN - 2, COLUMN))
    pair = (q, p + 1 - 2 * lax.rem(p, 2))

    fetch = pltpu.make_async_copy(shapes_hbm, shapes, shapes_sem)
    fetch.start()

    barrier = pltpu.get_barrier_semaphore()

    def greet_column(d, carry):
        pl.semaphore_signal(barrier, inc=1, device_id=(q, lax.rem(p + d, COLUMN)), device_id_type=MESH)
        return carry

    def greet_plane(d, carry):
        pl.semaphore_signal(barrier, inc=1, device_id=(lax.rem(q + d, PLANE), p), device_id_type=MESH)
        return carry

    lax.fori_loop(1, PLANE, greet_plane, 0)
    lax.fori_loop(1, COLUMN, greet_column, 0)

    resp = resp_ref[...].astype(F32).reshape(PLANE, 8, WIDTH)
    adjo = adjo_ref[...].astype(F32)
    odd = lax.broadcasted_iota(jnp.int32, adjo.shape, 0) % 2 == 1
    rows = adjo.shape[0]
    swapped = jnp.where(odd, -pltpu.roll(adjo, 1, 0), pltpu.roll(adjo, rows - 1, 0)).reshape(PLANE, 8, WIDTH)
    staged[...] = jnp.concatenate([resp, swapped], axis=1).astype(BF16)
    for x in quarters:
        x[PLANE] = jnp.zeros(x.shape[1:], BF16)
    x0[q, 0, 0] = staged[q]

    pl.semaphore_wait(barrier, PLANE - 1 + COLUMN - 1)

    def mix(d):
        there = lax.rem(q + d, PLANE)
        return pltpu.make_async_remote_copy(
            src_ref=staged.at[there],
            dst_ref=x0.at[q, 0, 0],
            send_sem=mix_send.at[d - 1],
            recv_sem=mix_recv,
            device_id=(there, p),
            device_id_type=MESH,
        )

    def mix_start(d, carry):
        mix(d).start()
        return carry

    lax.fori_loop(1, PLANE, mix_start, 0)

    owner_row = owner_ref[...].astype(F32)
    eye = lax.broadcasted_iota(jnp.int32, (PATCHES, PATCHES), 0) == lax.broadcasted_iota(jnp.int32, (PATCHES, PATCHES), 1)
    owner_column = jnp.sum(jnp.where(eye, jnp.broadcast_to(owner_row, (PATCHES, PATCHES)), 0.0), axis=1, keepdims=True)
    first = lax.broadcasted_iota(jnp.int32, (COLUMN, PATCHES), 0).astype(F32) * PATCHES
    owner_rows = jnp.broadcast_to(owner_row, (COLUMN, PATCHES))
    to_device = jnp.where((owner_rows >= first) & (owner_rows < first + PATCHES), 1.0, 0.0).astype(BF16)
    place = owner_column - jnp.floor((owner_column + 0.5) * (1.0 / PATCHES)) * PATCHES
    lane = lax.broadcasted_iota(jnp.int32, (PATCHES, WIDTH), 1).astype(F32)
    to_lane = jnp.where(place == lane, 1.0, 0.0)

    def chunk(core, slot, part=None):
        x = quarters[slot // QUARTERS]
        blocks = pl.ds(0, PLANE) if part is None else pl.ds(part * (PLANE // 2), PLANE // 2)
        return x.at[blocks, core, slot % QUARTERS]

    def to_right(hop, part):
        source = 0 if hop == 1 else from_left(hop - 1)
        target = from_left(hop) if hop < HOPS else 2 * HOPS - 1
        return pltpu.make_async_remote_copy(
            src_ref=chunk(0, source, part),
            dst_ref=chunk(0, target, part),
            send_sem=right_send.at[hop - 1, part],
            recv_sem=right_recv.at[hop - 1, part],
            device_id=right,
            device_id_type=MESH,
        )

    def to_left(hop, part):
        source = 0 if hop == 1 else from_right(hop - 1)
        target = from_right(hop) if hop < HOPS else 2 * HOPS - 1
        return pltpu.make_async_remote_copy(
            src_ref=chunk(0, source, part),
            dst_ref=chunk(0, target, part),
            send_sem=left_send.at[hop - 1, part],
            recv_sem=left_recv.at[hop - 1, part],
            device_id=left,
            device_id_type=MESH,
        )

    def to_pair(slot):
        return pltpu.make_async_remote_copy(
            src_ref=chunk(0, slot),
            dst_ref=chunk(1, slot),
            send_sem=pair_send.at[slot],
            recv_sem=pair_recv.at[slot],
            device_id=pair,
            device_id_type=MESH,
        )

    def goes_right(hop, part):
        return hop < HOPS or (hop == HOPS and part == 0)

    def goes_left(hop, part):
        return hop < HOPS or (hop == HOPS and part == 1)

    sample = lax.broadcasted_iota(jnp.int32, (SAMPLES, WIDTH), 0)

    def patch(quarter, index):
        x = quarters[quarter]
        live = counts_ref[index]
        sides = []
        for k in range(SLOTS):
            block = jnp.where(k < live, lists_ref[index * SLOTS + k], PLANE)
            sides.append(x[block].reshape(WIDTH, WIDTH))
        columns = jnp.concatenate(sides, axis=1)
        strain = jnp.concatenate([shapes[index, k] for k in range(SLOTS)], axis=1)
        both = lax.dot_general(strain, columns, (((1,), (1,)), ((), ())), preferred_element_type=F32)
        cross = both * pltpu.roll(both, WIDTH - 8, 1)
        cross = jnp.where(sample < sizes_ref[index], cross, 0.0)
        part = jnp.sum(cross.reshape(SAMPLES // 8, 8, WIDTH), axis=0)
        if quarter == 0:
            acc[index] = part
        elif quarter < QUARTERS - 1:
            acc[index] += part
        else:
            folded[index] = jnp.sum(acc[index] + part, axis=0, keepdims=True)

    def work(quarter, share, shares):
        turns = PATCHES // UNROLL // shares

        def turn(step, carry):
            for u in range(UNROLL):
                patch(quarter, step * UNROLL + u)
            return carry

        lax.fori_loop(share * turns, (share + 1) * turns, turn, 0)

    def mix_wait():
        pltpu.make_async_copy(x0.at[pl.ds(0, PLANE - 1), 0, 0], x0.at[pl.ds(0, PLANE - 1), 0, 0], mix_recv).wait()

    mix_wait()
    for part in range(2):
        to_right(1, part).start()
        to_left(1, part).start()
    to_pair(0).start()
    fetch.wait()

    queue = []
    for hop in range(1, HOPS + 1):
        for part in range(2):
            if goes_right(hop, part):
                to_right(hop, part).wait_recv()
                if goes_right(hop + 1, part):
                    to_right(hop + 1, part).start()
            if goes_left(hop, part):
                to_left(hop, part).wait_recv()
                if goes_left(hop + 1, part):
                    to_left(hop + 1, part).start()
            if part == 1:
                slots = (from_left(hop), from_right(hop)) if hop < HOPS else (2 * HOPS - 1,)
                for slot in slots:
                    to_pair(slot).start()
                    if slot % QUARTERS == QUARTERS - 1:
                        queue.extend((slot // QUARTERS, share) for share in range(4))
            if queue:
                quarter, share = queue.pop(0)
                if share == 0:
                    for slot in range(quarter * QUARTERS, (quarter + 1) * QUARTERS):
                        to_pair(slot).wait_recv()
                work(quarter, share, 4)
    while queue:
        quarter, share = queue.pop(0)
        if share == 0:
            for slot in range(quarter * QUARTERS, (quarter + 1) * QUARTERS):
                to_pair(slot).wait_recv()
            shares = 1
            queue = [entry for entry in queue if entry[0] != quarter]
            work(quarter, 0, 1)
        else:
            work(quarter, share, 4)

    lanes = lax.broadcasted_iota(jnp.int32, (PATCHES, WIDTH), 1)
    terms = jnp.where(lanes // 8 % 2 == 0, folded[...].reshape(PATCHES, WIDTH), 0.0)
    terms = jnp.sum(terms, axis=1, keepdims=True) * scale
    spread = terms * to_lane
    high = spread.astype(BF16)
    rest = spread - high.astype(F32)
    middle = rest.astype(BF16)
    low = (rest - middle.astype(F32)).astype(BF16)
    placed = sum(
        lax.dot_general(to_device, piece, (((1,), (0,)), ((), ())), preferred_element_type=F32)
        for piece in (low, middle, high)
    )
    dense[...] = placed.reshape(COLUMN, 1, WIDTH)

    def column(d):
        there = lax.rem(p + d, COLUMN)
        return pltpu.make_async_remote_copy(
            src_ref=dense.at[there],
            dst_ref=got_column.at[d - 1],
            send_sem=column_send.at[d - 1],
            recv_sem=column_recv,
            device_id=(q, there),
            device_id_type=MESH,
        )

    def column_start(d, carry):
        column(d).start()
        return carry

    lax.fori_loop(1, COLUMN, column_start, 0)
    pltpu.make_async_copy(got_column, got_column, column_recv).wait()
    row[...] = dense[p] + jnp.sum(got_column[...], axis=0)

    def plane(d):
        return pltpu.make_async_remote_copy(
            src_ref=row,
            dst_ref=got_plane.at[d - 1],
            send_sem=plane_send.at[d - 1],
            recv_sem=plane_recv,
            device_id=(lax.rem(q + d, PLANE), p),
            device_id_type=MESH,
        )

    def plane_start(d, carry):
        plane(d).start()
        return carry

    lax.fori_loop(1, PLANE, plane_start, 0)
    pltpu.make_async_copy(got_plane, got_plane, plane_recv).wait()
    total = row[...] + jnp.sum(got_plane[...], axis=0)
    out_ref[...] = total[:, :PATCHES]

    def mix_sent(d, carry):
        mix(d).wait_send()
        return carry

    def column_sent(d, carry):
        column(d).wait_send()
        return carry

    def plane_sent(d, carry):
        plane(d).wait_send()
        return carry

    lax.fori_loop(1, PLANE, mix_sent, 0)
    for hop in range(1, HOPS + 1):
        for part in range(2):
            if goes_right(hop, part):
                to_right(hop, part).wait_send()
            if goes_left(hop, part):
                to_left(hop, part).wait_send()
    for slot in range(2 * HOPS):
        to_pair(slot).wait_send()
    lax.fori_loop(1, COLUMN, column_sent, 0)
    lax.fori_loop(1, PLANE, plane_sent, 0)


def body(responses, adjoints, patch_shapes, block_lists, block_counts, patch_sizes, owner_map):
    freqs = responses.shape[0] * COLUMN
    scale = (SAMPLES * freqs) ** (-0.5)
    vmem = pl.BlockSpec(memory_space=pltpu.VMEM)
    smem = pl.BlockSpec(memory_space=pltpu.SMEM)
    quarter = pltpu.VMEM((PLANE + 1, 2, QUARTERS, PIECE, WIDTH), BF16)
    dma = pltpu.SemaphoreType.DMA
    rows = responses.shape[0] * 2
    out = pl.pallas_call(
        functools.partial(kernel, scale),
        out_shape=jax.ShapeDtypeStruct((1, PATCHES), F32),
        in_specs=[vmem, vmem, smem, smem, smem, vmem, pl.BlockSpec(memory_space=pl.ANY)],
        out_specs=vmem,
        scratch_shapes=[
            pltpu.VMEM((PLANE, PIECE, WIDTH), BF16),
            quarter,
            quarter,
            quarter,
            quarter,
            pltpu.VMEM(patch_shapes.shape, BF16),
            pltpu.VMEM((PATCHES, 8, WIDTH), F32),
            pltpu.VMEM((PATCHES, 1, WIDTH), F32),
            pltpu.VMEM((COLUMN, 1, WIDTH), F32),
            pltpu.VMEM((COLUMN - 1, 1, WIDTH), F32),
            pltpu.VMEM((1, WIDTH), F32),
            pltpu.VMEM((PLANE - 1, 1, WIDTH), F32),
            dma,
            dma((PLANE - 1,)),
            dma,
            dma((HOPS, 2)),
            dma((HOPS, 2)),
            dma((HOPS, 2)),
            dma((HOPS, 2)),
            dma((2 * HOPS,)),
            dma((2 * HOPS,)),
            dma((COLUMN - 1,)),
            dma,
            dma((PLANE - 1,)),
            dma,
        ],
        compiler_params=pltpu.CompilerParams(
            collective_id=0, has_side_effects=True, vmem_limit_bytes=32 * 1024 * 1024
        ),
        cost_estimate=pl.CostEstimate(flops=2415919104, bytes_accessed=5000000, transcendentals=0),
    )(
        responses.reshape(rows, WIDTH),
        adjoints.reshape(rows, WIDTH),
        block_lists.reshape(-1),
        block_counts,
        patch_sizes,
        owner_map.reshape(1, -1),
        patch_shapes,
    )
    return out.reshape(-1)


def solution(mesh):
    placed = (
        P("patch", None, "freq"),
        P("patch", None, "freq"),
        P("patch", None, None, None),
        P("patch", None),
        P("patch"),
        P("patch"),
        P("patch"),
    )
    return jax.shard_map(body, mesh=mesh, in_specs=placed, out_specs=P("patch"), check_vma=False)
```

time: 487 us -> 81.7 us (0.17); the launches traced: 480 us -> 81.4 us
  blocking collectives: 147 us -> 0 us
  local copies, waits for them, and re-layouts: 133 us -> 7.21 us
  waiting for transfers between devices: 122 us -> 0 us
  Pallas kernels: 0 us -> 74.2 us
  matrix products: 47.9 us -> 0 us
  other arithmetic: 16.3 us -> 0 us
  between operations: 14.1 us -> 0.03 us
    all_gather x2 -> x0, waiting for transfers between devices: 122 us -> none  [the longest x1 70 us: body(): lax.all_gather(regrouped[1], 'patch', axis=0, tiled=True)]
    gather x8 -> x0, local copies, waits for them, and re-layouts: 107 us -> none  [the longest x4 53.3 us: one(): resp[:, blocks, :]]
    unnamed x1 -> x0, blocking collectives: 89.1 us -> none
    pallas_call x0 -> x1, Pallas kernels: none -> 74.2 us  [body(): pl.pallas_call(functools.partial(kernel, scale), out_shape=jax.ShapeDtype...]
    dot_general x9 -> x0, matrix products: 47.9 us -> none  [the longest x4 23.7 us: one(): jnp.einsum('pksb,cpkb->cps', masked, adjo[:, blocks, :], preferred_elemen...]
    psum x1 -> x0, blocking collectives: 33.7 us -> none  [body(): return lax.psum(mine, 'freq')]
    all_to_all x2 -> x0, blocking collectives: 23.9 us -> none  [the longest x1 14 us: body(): lax.all_to_all(responses, 'freq', split_axis=0, concat_axis=2, tiled=True)]
    transpose x8 -> x0, local copies, waits for them, and re-layouts: 14.9 us -> none  [the longest x4 7.48 us: one(): jnp.einsum('pksb,cpkb->cps', masked, adjo[:, blocks, :], preferred_elemen...]
  transfers between devices with their start and end apart: 2 -> 0, of which waited for: 2 -> 0; matrix products, arithmetic and copies ran while one was open for 2% -> 0% of each run, Pallas kernels for 0% -> 0%
where the time goes in v1:
time: 81.7 us; the launch traced here: 81.4 us
  Pallas kernels  74.2 us (91%)
  local copies, waits for them, and re-layouts  7.21 us (9%)
    pallas_call x1, Pallas kernels, body(): pl.pallas_call(functools.partial(kernel, scale), out_shape=jax.ShapeDtype...  74.2 us
    unnamed x14, local copies, waits for them, and re-layouts  7.1 us

profile of v1, /device:TPU:1, one launch (start us, length us, event | category | flops | bytes accessed | tf_op | source)
XLA Modules:
  0.0 81.4 jit_solution(307003558349161027)
XLA Ops:
  0.0 0.8 copy.8
  0.8 0.1 reshape.17.lists_ref
  0.9 0.0 copy-start
  0.9 2.3 %copy-done = bf16[96,4,48,128]{3,2,1,0:T(8,128)(2,1)S(1)} copy-done((bf16[96,4,48,128]{3,2,1,0:T(8,128)(2,1)S(1)}, bf16[96,4,48,128]{3,2,1,0:T(8,128)(2,1)}, u32[]{:S(2)}) %copy-start) | copy-done | bytes 4718616
  3.2 0.0 copy-start.1
  3.2 0.8 copy-done.1
  4.0 0.0 copy-start.2
  4.0 0.8 copy-done.2
  4.7 0.0 copy-start.3
  4.7 0.7 copy-done.3
  5.4 0.0 copy-start.4
  5.4 0.7 copy-done.4
  6.1 0.0 copy-start.5
  6.1 0.7 copy-done.5
  6.7 74.2 %shard_map.73 = f32[1,96]{1,0:T(1,128)S(1)} custom-call(bf16[128,128]{1,0:T(8,128)(2,1)S(1)} %bitcast.4, bf16[128,128]{1,0:T(8,128)(2,1)S(1)} %bitcast.5, s32[384]{0:T(512)S(1)} %reshape.17.lists_ref, s32[96]{0:T(128)S(1)} %copy-done.3, s32[96]{0:T(128)S(1)} %copy-done.4, s32[1,96]{1,0:T(1,128)S(1)} %bitcast.6, bf16[96,4,48,128]{3,2,1,0:T(8,128)(2,1)S(1)} %copy-done), custom_call_target="tpu_custom_call" | custom-call | flops 2415919104 | bytes 5000000 | tf_op jit(solution)/shard_map/pallas_call | solution.py:339
  80.9 0.5 copy.10
Async XLA Ops:
  0.9 2.3 %copy-start = (bf16[96,4,48,128]{3,2,1,0:T(8,128)(2,1)S(1)}, bf16[96,4,48,128]{3,2,1,0:T(8,128)(2,1)}, u32[]{:S(2)}) copy-start(bf16[96,4,48,128]{3,2,1,0:T(8,128)(2,1)} %shapes_hbm.1) | copy-start | bytes 14155780
  3.2 0.8 copy-start.1
  4.0 0.8 copy-start.2
  4.7 0.7 copy-start.3
  5.4 0.7 copy-start.4
  6.1 0.7 copy-start.5

commit v2 on v1

--- a/solution.py
+++ b/solution.py
@@ -14,22 +14,26 @@
 PLANE = 16
 COLUMN = 32
 RING = 16
-HOPS = 8
 PATCHES = 96
 SLOTS = 4
 SAMPLES = 48
 WIDTH = 128
 PIECE = 16
 QUARTERS = 4
-UNROLL = 8
-
-
-def from_left(hop):
-    return 2 * hop - 1
-
-
-def from_right(hop):
-    return 2 * hop
+UNROLL = 16
+
+
+EDGES = ((0, 1), (0, 3), (1, 2), (3, 4), (3, 6), (4, 5), (6, 7), (7, 8))
+FAR = RING // 2
+ARRIVAL = (1, 3, 2, 4, 6, 5, 7)
+
+
+def slot_of(distance, side):
+    if distance == 0:
+        return 0
+    if distance == FAR:
+        return 2 * FAR - 1
+    return 1 + 2 * ARRIVAL.index(distance) + side
 
 
 def kernel(
@@ -47,6 +51,8 @@
     x1,
     x2,
     x3,
+    turned0,
+    turned1,
     shapes,
     acc,
     folded,
@@ -57,10 +63,10 @@
     shapes_sem,
     mix_send,
     mix_recv,
-    right_send,
-    left_send,
-    right_recv,
-    left_recv,
+    ring_send,
+    ring_recv,
+    far_send,
+    far_recv,
     pair_send,
     pair_recv,
     column_send,
@@ -69,10 +75,9 @@
     plane_recv,
 ):
     quarters = (x0, x1, x2, x3)
+    halves = (turned0, turned1)
     q = lax.axis_index("freq")
     p = lax.axis_index("patch")
-    right = (q, lax.rem(p + 2, COLUMN))
-    left = (q, lax.rem(p + COLUMN - 2, COLUMN))
     pair = (q, p + 1 - 2 * lax.rem(p, 2))
 
     fetch = pltpu.make_async_copy(shapes_hbm, shapes, shapes_sem)
@@ -97,8 +102,8 @@
     rows = adjo.shape[0]
     swapped = jnp.where(odd, -pltpu.roll(adjo, 1, 0), pltpu.roll(adjo, rows - 1, 0)).reshape(PLANE, 8, WIDTH)
     staged[...] = jnp.concatenate([resp, swapped], axis=1).astype(BF16)
-    for x in quarters:
-        x[PLANE] = jnp.zeros(x.shape[1:], BF16)
+    for turned in halves:
+        turned[PLANE] = jnp.zeros(turned.shape[1:], BF16)
     x0[q, 0, 0] = staged[q]
 
     pl.semaphore_wait(barrier, PLANE - 1 + COLUMN - 1)
@@ -135,27 +140,26 @@
         blocks = pl.ds(0, PLANE) if part is None else pl.ds(part * (PLANE // 2), PLANE // 2)
         return x.at[blocks, core, slot % QUARTERS]
 
-    def to_right(hop, part):
-        source = 0 if hop == 1 else from_left(hop - 1)
-        target = from_left(hop) if hop < HOPS else 2 * HOPS - 1
-        return pltpu.make_async_remote_copy(
-            src_ref=chunk(0, source, part),
-            dst_ref=chunk(0, target, part),
-            send_sem=right_send.at[hop - 1, part],
-            recv_sem=right_recv.at[hop - 1, part],
-            device_id=right,
-            device_id_type=MESH,
-        )
-
-    def to_left(hop, part):
-        source = 0 if hop == 1 else from_right(hop - 1)
-        target = from_right(hop) if hop < HOPS else 2 * HOPS - 1
-        return pltpu.make_async_remote_copy(
-            src_ref=chunk(0, source, part),
-            dst_ref=chunk(0, target, part),
-            send_sem=left_send.at[hop - 1, part],
-            recv_sem=left_recv.at[hop - 1, part],
-            device_id=left,
+    def along(side, edge, part):
+        near, far = EDGES[edge]
+        step = 2 * (far - near) * (1 - 2 * side)
+        return pltpu.make_async_remote_copy(
+            src_ref=chunk(0, slot_of(near, side), part),
+            dst_ref=chunk(0, slot_of(far, side), part),
+            send_sem=ring_send.at[side, edge, part],
+            recv_sem=ring_recv.at[side, edge, part],
+            device_id=(q, lax.rem(p + COLUMN + step, COLUMN)),
+            device_id_type=MESH,
+        )
+
+    def to_far_pair(side):
+        last = slot_of(FAR, side)
+        return pltpu.make_async_remote_copy(
+            src_ref=chunk(0, slot_of(FAR - 1, side), side),
+            dst_ref=chunk(1, last, side),
+            send_sem=far_send.at[side],
+            recv_sem=far_recv.at[side],
+            device_id=(q, lax.rem(pair[1] + COLUMN + 2 * (1 - 2 * side), COLUMN)),
             device_id_type=MESH,
         )
 
@@ -169,87 +173,96 @@
             device_id_type=MESH,
         )
 
-    def goes_right(hop, part):
-        return hop < HOPS or (hop == HOPS and part == 0)
-
-    def goes_left(hop, part):
-        return hop < HOPS or (hop == HOPS and part == 1)
+    def taken(side, edge, part):
+        return EDGES[edge][1] < FAR or part == side
+
+    def send_on(side, distance, part):
+        for edge, (near, far) in enumerate(EDGES):
+            if near == distance and taken(side, edge, part):
+                along(side, edge, part).start()
+                if far == FAR:
+                    to_far_pair(side).start()
 
     sample = lax.broadcasted_iota(jnp.int32, (SAMPLES, WIDTH), 0)
 
-    def patch(quarter, index):
-        x = quarters[quarter]
+    def patch(half, index):
         live = counts_ref[index]
         sides = []
         for k in range(SLOTS):
-            block = jnp.where(k < live, lists_ref[index * SLOTS + k], PLANE)
-            sides.append(x[block].reshape(WIDTH, WIDTH))
-        columns = jnp.concatenate(sides, axis=1)
+            block = jnp.where(k < live, lists_ref[k, index], PLANE)
+            sides.append(halves[half][block])
+        columns = jnp.concatenate(sides, axis=0)
         strain = jnp.concatenate([shapes[index, k] for k in range(SLOTS)], axis=1)
-        both = lax.dot_general(strain, columns, (((1,), (1,)), ((), ())), preferred_element_type=F32)
-        cross = both * pltpu.roll(both, WIDTH - 8, 1)
+        both = jnp.dot(strain, columns, preferred_element_type=F32)
+        cross = 0.0
+        for at in (0, WIDTH):
+            part = both[:, at : at + WIDTH]
+            cross = cross + part * pltpu.roll(part, WIDTH - 8, 1)
         cross = jnp.where(sample < sizes_ref[index], cross, 0.0)
         part = jnp.sum(cross.reshape(SAMPLES // 8, 8, WIDTH), axis=0)
-        if quarter == 0:
+        if half == 0:
             acc[index] = part
-        elif quarter < QUARTERS - 1:
-            acc[index] += part
         else:
             folded[index] = jnp.sum(acc[index] + part, axis=0, keepdims=True)
 
-    def work(quarter, share, shares):
+    def work(half, share, shares):
         turns = PATCHES // UNROLL // shares
 
         def turn(step, carry):
             for u in range(UNROLL):
-                patch(quarter, step * UNROLL + u)
+                patch(half, step * UNROLL + u)
             return carry
 
         lax.fori_loop(share * turns, (share + 1) * turns, turn, 0)
 
-    def mix_wait():
-        pltpu.make_async_copy(x0.at[pl.ds(0, PLANE - 1), 0, 0], x0.at[pl.ds(0, PLANE - 1), 0, 0], mix_recv).wait()
-
-    mix_wait()
+    def pair_wait(slot):
+        if slot == 2 * FAR - 1:
+            for side in range(2):
+                to_far_pair(side).wait_recv()
+        else:
+            to_pair(slot).wait_recv()
+
+    def turn_over(quarter):
+        for slot in range(quarter * QUARTERS, (quarter + 1) * QUARTERS):
+            pair_wait(slot)
+        x = quarters[quarter]
+        turned = halves[quarter // 2]
+        at = quarter % 2 * WIDTH
+
+        def block(b, carry):
+            turned[b, :, at : at + WIDTH] = x[b].reshape(WIDTH, WIDTH).T
+            return carry
+
+        lax.fori_loop(0, PLANE, block, 0)
+
+    pltpu.make_async_copy(x0.at[pl.ds(0, PLANE - 1), 0, 0], x0.at[pl.ds(0, PLANE - 1), 0, 0], mix_recv).wait()
     for part in range(2):
-        to_right(1, part).start()
-        to_left(1, part).start()
+        for side in range(2):
+            send_on(side, 0, part)
     to_pair(0).start()
-    fetch.wait()
-
-    queue = []
-    for hop in range(1, HOPS + 1):
+
+    tasks = {
+        2: [lambda: turn_over(0), fetch.wait],
+        4: [lambda: turn_over(1), lambda: work(0, 0, 6)],
+        5: [lambda: work(0, 1, 6), lambda: work(0, 2, 6)],
+        6: [lambda: work(0, 3, 6), lambda: turn_over(2), lambda: work(0, 4, 6), lambda: work(0, 5, 6)],
+    }
+    for edge, (_, far) in enumerate(EDGES):
+        pending = list(tasks.get(edge, ()))
         for part in range(2):
-            if goes_right(hop, part):
-                to_right(hop, part).wait_recv()
-                if goes_right(hop + 1, part):
-                    to_right(hop + 1, part).start()
-            if goes_left(hop, part):
-                to_left(hop, part).wait_recv()
-                if goes_left(hop + 1, part):
-                    to_left(hop + 1, part).start()
-            if part == 1:
-                slots = (from_left(hop), from_right(hop)) if hop < HOPS else (2 * HOPS - 1,)
-                for slot in slots:
-                    to_pair(slot).start()
-                    if slot % QUARTERS == QUARTERS - 1:
-                        queue.extend((slot // QUARTERS, share) for share in range(4))
-            if queue:
-                quarter, share = queue.pop(0)
-                if share == 0:
-                    for slot in range(quarter * QUARTERS, (quarter + 1) * QUARTERS):
-                        to_pair(slot).wait_recv()
-                work(quarter, share, 4)
-    while queue:
-        quarter, share = queue.pop(0)
-        if share == 0:
-            for slot in range(quarter * QUARTERS, (quarter + 1) * QUARTERS):
-                to_pair(slot).wait_recv()
-            shares = 1
-            queue = [entry for entry in queue if entry[0] != quarter]
-            work(quarter, 0, 1)
-        else:
-            work(quarter, share, 4)
+            for side in range(2):
+                if taken(side, edge, part):
+                    along(side, edge, part).wait_recv()
+                    if far < FAR:
+                        send_on(side, far, part)
+                        if part == 1:
+                            to_pair(slot_of(far, side)).start()
+            if part == 0 and len(pending) > 1 and edge > 3:
+                pending.pop(0)()
+        for task in pending:
+            task()
+    turn_over(3)
+    work(1, 0, 1)
 
     lanes = lax.broadcasted_iota(jnp.int32, (PATCHES, WIDTH), 1)
     terms = jnp.where(lanes // 8 % 2 == 0, folded[...].reshape(PATCHES, WIDTH), 0.0)
@@ -265,7 +278,8 @@
     )
     dense[...] = placed.reshape(COLUMN, 1, WIDTH)
 
-    def column(d):
+    def column(i):
+        d = COLUMN // 2 + (1 - 2 * lax.rem(i, 2)) * lax.div(i, 2)
         there = lax.rem(p + d, COLUMN)
         return pltpu.make_async_remote_copy(
             src_ref=dense.at[there],
@@ -316,13 +330,14 @@
         return carry
 
     lax.fori_loop(1, PLANE, mix_sent, 0)
-    for hop in range(1, HOPS + 1):
+    for edge in range(len(EDGES)):
         for part in range(2):
-            if goes_right(hop, part):
-                to_right(hop, part).wait_send()
-            if goes_left(hop, part):
-                to_left(hop, part).wait_send()
-    for slot in range(2 * HOPS):
+            for side in range(2):
+                if taken(side, edge, part):
+                    along(side, edge, part).wait_send()
+    for side in range(2):
+        to_far_pair(side).wait_send()
+    for slot in range(2 * FAR - 1):
         to_pair(slot).wait_send()
     lax.fori_loop(1, COLUMN, column_sent, 0)
     lax.fori_loop(1, PLANE, plane_sent, 0)
@@ -333,7 +348,7 @@
     scale = (SAMPLES * freqs) ** (-0.5)
     vmem = pl.BlockSpec(memory_space=pltpu.VMEM)
     smem = pl.BlockSpec(memory_space=pltpu.SMEM)
-    quarter = pltpu.VMEM((PLANE + 1, 2, QUARTERS, PIECE, WIDTH), BF16)
+    quarter = pltpu.VMEM((PLANE, 2, QUARTERS, PIECE, WIDTH), BF16)
     dma = pltpu.SemaphoreType.DMA
     rows = responses.shape[0] * 2
     out = pl.pallas_call(
@@ -347,6 +362,8 @@
             quarter,
             quarter,
             quarter,
+            pltpu.VMEM((PLANE + 1, WIDTH, 2 * WIDTH), BF16),
+            pltpu.VMEM((PLANE + 1, WIDTH, 2 * WIDTH), BF16),
             pltpu.VMEM(patch_shapes.shape, BF16),
             pltpu.VMEM((PATCHES, 8, WIDTH), F32),
             pltpu.VMEM((PATCHES, 1, WIDTH), F32),
@@ -357,25 +374,25 @@
             dma,
             dma((PLANE - 1,)),
             dma,
-            dma((HOPS, 2)),
-            dma((HOPS, 2)),
-            dma((HOPS, 2)),
-            dma((HOPS, 2)),
-            dma((2 * HOPS,)),
-            dma((2 * HOPS,)),
+            dma((2, len(EDGES), 2)),
+            dma((2, len(EDGES), 2)),
+            dma((2,)),
+            dma((2,)),
+            dma((2 * FAR - 1,)),
+            dma((2 * FAR - 1,)),
             dma((COLUMN - 1,)),
             dma,
             dma((PLANE - 1,)),
             dma,
         ],
         compiler_params=pltpu.CompilerParams(
-            collective_id=0, has_side_effects=True, vmem_limit_bytes=32 * 1024 * 1024
+            collective_id=0, has_side_effects=True, vmem_limit_bytes=58 * 1024 * 1024
         ),
         cost_estimate=pl.CostEstimate(flops=2415919104, bytes_accessed=5000000, transcendentals=0),
     )(
         responses.reshape(rows, WIDTH),
         adjoints.reshape(rows, WIDTH),
-        block_lists.reshape(-1),
+        block_lists.T,
         block_counts,
         patch_sizes,
         owner_map.reshape(1, -1),

time: 81.7 us -> 67.3 us (0.82)
  Pallas kernels: 74.2 us -> 65.9 us
  local copies, waits for them, and re-layouts: 7.21 us -> 1.19 us
    pallas_call x1, Pallas kernels: 74.2 us -> 65.9 us  [body(): pl.pallas_call(functools.partial(kernel, scale), out_shape=jax.ShapeDtype...]
    unnamed x14 -> x1, local copies, waits for them, and re-layouts: 7.1 us -> 1.19 us
where the time goes in v2:
time: 67.3 us; the launch traced here: 67.1 us
  Pallas kernels  65.9 us (98%)
  local copies, waits for them, and re-layouts  1.19 us (2%)
    pallas_call x1, Pallas kernels, body(): pl.pallas_call(functools.partial(kernel, scale), out_shape=jax.ShapeDtype...  65.9 us

profile of v2, /device:TPU:1, one launch (start us, length us, event | category | flops | bytes accessed | tf_op | source)
XLA Modules:
  0.0 67.1 jit_solution(7053787358667385209)
XLA Ops:
  0.0 65.9 %shard_map.73 = f32[1,96]{1,0:T(1,128)} custom-call(bf16[128,128]{1,0:T(8,128)(2,1)} %bitcast.5, bf16[128,128]{1,0:T(8,128)(2,1)} %bitcast.6, s32[4,96]{1,0:T(4,128)} %bitcast.7, s32[96]{0:T(128)} %counts_ref.1, s32[96]{0:T(128)} %sizes_ref.1, s32[1,96]{1,0:T(1,128)} %bitcast.8, bf16[96,4,48,128]{3,2,1,0:T(8,128)(2,1)} %shapes_hbm.1), custom_call_target="tpu_custom_call" | custom-call | flops 2415919104 | bytes 5000000 | tf_op jit(solution)/shard_map/pallas_call | solution.py:354
  65.9 1.2 %copy.9 = f32[96]{0:T(128)} copy(f32[96]{0:T(128)} %bitcast.9) | data formatting | bytes 768

commit v3 on v2

--- a/solution.py
+++ b/solution.py
@@ -23,9 +23,10 @@
 UNROLL = 16
 
 
-EDGES = ((0, 1), (0, 3), (1, 2), (3, 4), (3, 6), (4, 5), (6, 7), (7, 8))
+EDGES = ((2, 3), (2, 5), (3, 4), (5, 6), (6, 7), (7, 8))
+REACH = 2
 FAR = RING // 2
-ARRIVAL = (1, 3, 2, 4, 6, 5, 7)
+ARRIVAL = (1, 2, 3, 5, 4, 6, 7)
 
 
 def slot_of(distance, side):
@@ -38,14 +39,21 @@
 
 def kernel(
     scale,
+    resp_hbm,
+    adjo_hbm,
+    lists_hbm,
+    counts_hbm,
+    sizes_hbm,
+    owner_hbm,
+    shapes_hbm,
+    out_ref,
     resp_ref,
     adjo_ref,
     lists_ref,
     counts_ref,
     sizes_ref,
     owner_ref,
-    shapes_hbm,
-    out_ref,
+    input_sem,
     staged,
     x0,
     x1,
@@ -60,7 +68,6 @@
     got_column,
     row,
     got_plane,
-    shapes_sem,
     mix_send,
     mix_recv,
     ring_send,
@@ -80,21 +87,45 @@
     p = lax.axis_index("patch")
     pair = (q, p + 1 - 2 * lax.rem(p, 2))
 
-    fetch = pltpu.make_async_copy(shapes_hbm, shapes, shapes_sem)
-    fetch.start()
+    planes = tuple(sorted(range(-REACH, REACH + 1), key=lambda dz: -abs(dz)))
+
+    def shifted(dz):
+        return lax.rem(p + COLUMN + 2 * dz, COLUMN)
+
+    inputs = [
+        pltpu.make_async_copy(source, target, input_sem.at[at])
+        for at, (source, target) in enumerate(
+            (
+                (resp_hbm, resp_ref),
+                (adjo_hbm, adjo_ref),
+                (owner_hbm, owner_ref),
+                (lists_hbm, lists_ref),
+                (counts_hbm, counts_ref),
+                (sizes_hbm, sizes_ref),
+                (shapes_hbm, shapes),
+            )
+        )
+    ]
+    for copy in inputs[:2]:
+        copy.start()
 
     barrier = pltpu.get_barrier_semaphore()
-
-    def greet_column(d, carry):
-        pl.semaphore_signal(barrier, inc=1, device_id=(q, lax.rem(p + d, COLUMN)), device_id_type=MESH)
-        return carry
-
-    def greet_plane(d, carry):
-        pl.semaphore_signal(barrier, inc=1, device_id=(lax.rem(q + d, PLANE), p), device_id_type=MESH)
-        return carry
-
-    lax.fori_loop(1, PLANE, greet_plane, 0)
-    lax.fori_loop(1, COLUMN, greet_column, 0)
+    greeted = 0
+    for dz in planes:
+
+        def greet(d, carry, dz=dz):
+            pl.semaphore_signal(barrier, inc=1, device_id=(lax.rem(q + d, PLANE), shifted(dz)), device_id_type=MESH)
+            return carry
+
+        lax.fori_loop(0 if dz else 1, PLANE, greet, 0)
+        greeted += PLANE if dz else PLANE - 1
+    for there in (pair, (q, shifted(3)), (q, shifted(-3)), (q, lax.rem(pair[1] + 2, COLUMN)), (q, lax.rem(pair[1] + COLUMN - 2, COLUMN))):
+        pl.semaphore_signal(barrier, inc=1, device_id=there, device_id_type=MESH)
+        greeted += 1
+    for copy in inputs[2:]:
+        copy.start()
+    for copy in inputs[:2]:
+        copy.wait()
 
     resp = resp_ref[...].astype(F32).reshape(PLANE, 8, WIDTH)
     adjo = adjo_ref[...].astype(F32)
@@ -102,28 +133,42 @@
     rows = adjo.shape[0]
     swapped = jnp.where(odd, -pltpu.roll(adjo, 1, 0), pltpu.roll(adjo, rows - 1, 0)).reshape(PLANE, 8, WIDTH)
     staged[...] = jnp.concatenate([resp, swapped], axis=1).astype(BF16)
+    x0[q, 0, 0] = staged[q]
+
+    pl.semaphore_wait(barrier, greeted)
+
+    def chunk(core, slot, part=None):
+        x = quarters[slot // QUARTERS]
+        blocks = pl.ds(0, PLANE) if part is None else pl.ds(part * (PLANE // 2), PLANE // 2)
+        return x.at[blocks, core, slot % QUARTERS]
+
+    def arrives(dz):
+        return slot_of(abs(dz), 0 if dz > 0 else 1)
+
+    for at, dz in enumerate(planes):
+
+        def mix_start(d, carry, at=at, dz=dz):
+            there = lax.rem(q + d, PLANE)
+            slot = arrives(dz)
+            pltpu.make_async_remote_copy(
+                src_ref=staged.at[there],
+                dst_ref=quarters[slot // QUARTERS].at[q, 0, slot % QUARTERS],
+                send_sem=mix_send.at[at],
+                recv_sem=mix_recv.at[at],
+                device_id=(there, shifted(dz)),
+                device_id_type=MESH,
+            ).start()
+            return carry
+
+        lax.fori_loop(0 if dz else 1, PLANE, mix_start, 0)
+
+    def mix_wait(at, dz, sems):
+        pieces = staged if dz else staged.at[pl.ds(0, PLANE - 1)]
+        pltpu.make_async_copy(pieces, pieces, sems.at[at]).wait()
+
     for turned in halves:
         turned[PLANE] = jnp.zeros(turned.shape[1:], BF16)
-    x0[q, 0, 0] = staged[q]
-
-    pl.semaphore_wait(barrier, PLANE - 1 + COLUMN - 1)
-
-    def mix(d):
-        there = lax.rem(q + d, PLANE)
-        return pltpu.make_async_remote_copy(
-            src_ref=staged.at[there],
-            dst_ref=x0.at[q, 0, 0],
-            send_sem=mix_send.at[d - 1],
-            recv_sem=mix_recv,
-            device_id=(there, p),
-            device_id_type=MESH,
-        )
-
-    def mix_start(d, carry):
-        mix(d).start()
-        return carry
-
-    lax.fori_loop(1, PLANE, mix_start, 0)
+    inputs[2].wait()
 
     owner_row = owner_ref[...].astype(F32)
     eye = lax.broadcasted_iota(jnp.int32, (PATCHES, PATCHES), 0) == lax.broadcasted_iota(jnp.int32, (PATCHES, PATCHES), 1)
@@ -134,11 +179,6 @@
     place = owner_column - jnp.floor((owner_column + 0.5) * (1.0 / PATCHES)) * PATCHES
     lane = lax.broadcasted_iota(jnp.int32, (PATCHES, WIDTH), 1).astype(F32)
     to_lane = jnp.where(place == lane, 1.0, 0.0)
-
-    def chunk(core, slot, part=None):
-        x = quarters[slot // QUARTERS]
-        blocks = pl.ds(0, PLANE) if part is None else pl.ds(part * (PLANE // 2), PLANE // 2)
-        return x.at[blocks, core, slot % QUARTERS]
 
     def along(side, edge, part):
         near, far = EDGES[edge]
@@ -206,11 +246,12 @@
             folded[index] = jnp.sum(acc[index] + part, axis=0, keepdims=True)
 
     def work(half, share, shares):
-        turns = PATCHES // UNROLL // shares
+        length = 2 * UNROLL if shares == 1 else UNROLL
+        turns = PATCHES // length // shares
 
         def turn(step, carry):
-            for u in range(UNROLL):
-                patch(half, step * UNROLL + u)
+            for u in range(length):
+                patch(half, step * length + u)
             return carry
 
         lax.fori_loop(share * turns, (share + 1) * turns, turn, 0)
@@ -233,19 +274,22 @@
             turned[b, :, at : at + WIDTH] = x[b].reshape(WIDTH, WIDTH).T
             return carry
 
-        lax.fori_loop(0, PLANE, block, 0)
-
-    pltpu.make_async_copy(x0.at[pl.ds(0, PLANE - 1), 0, 0], x0.at[pl.ds(0, PLANE - 1), 0, 0], mix_recv).wait()
-    for part in range(2):
-        for side in range(2):
-            send_on(side, 0, part)
-    to_pair(0).start()
+        lax.fori_loop(0, PLANE, block, 0, unroll=4)
+
+    for at, dz in enumerate(planes):
+        mix_wait(at, dz, mix_recv)
+        if abs(dz) == REACH:
+            for part in range(2):
+                send_on(0 if dz > 0 else 1, REACH, part)
+        to_pair(arrives(dz) if dz else 0).start()
+    for copy in inputs[3:]:
+        copy.wait()
 
     tasks = {
-        2: [lambda: turn_over(0), fetch.wait],
-        4: [lambda: turn_over(1), lambda: work(0, 0, 6)],
-        5: [lambda: work(0, 1, 6), lambda: work(0, 2, 6)],
-        6: [lambda: work(0, 3, 6), lambda: turn_over(2), lambda: work(0, 4, 6), lambda: work(0, 5, 6)],
+        1: [lambda: turn_over(0)],
+        2: [lambda: turn_over(1), lambda: work(0, 0, 6)],
+        3: [lambda: work(0, 1, 6), lambda: work(0, 2, 6)],
+        4: [lambda: work(0, 3, 6), lambda: turn_over(2), lambda: work(0, 4, 6), lambda: work(0, 5, 6)],
     }
     for edge, (_, far) in enumerate(EDGES):
         pending = list(tasks.get(edge, ()))
@@ -257,7 +301,7 @@
                         send_on(side, far, part)
                         if part == 1:
                             to_pair(slot_of(far, side)).start()
-            if part == 0 and len(pending) > 1 and edge > 3:
+            if part == 0 and len(pending) > 1 and edge > 2:
                 pending.pop(0)()
         for task in pending:
             task()
@@ -317,10 +361,6 @@
     total = row[...] + jnp.sum(got_plane[...], axis=0)
     out_ref[...] = total[:, :PATCHES]
 
-    def mix_sent(d, carry):
-        mix(d).wait_send()
-        return carry
-
     def column_sent(d, carry):
         column(d).wait_send()
         return carry
@@ -329,7 +369,8 @@
         plane(d).wait_send()
         return carry
 
-    lax.fori_loop(1, PLANE, mix_sent, 0)
+    for at, dz in enumerate(planes):
+        mix_wait(at, dz, mix_send)
     for edge in range(len(EDGES)):
         for part in range(2):
             for side in range(2):
@@ -347,16 +388,22 @@
     freqs = responses.shape[0] * COLUMN
     scale = (SAMPLES * freqs) ** (-0.5)
     vmem = pl.BlockSpec(memory_space=pltpu.VMEM)
-    smem = pl.BlockSpec(memory_space=pltpu.SMEM)
     quarter = pltpu.VMEM((PLANE, 2, QUARTERS, PIECE, WIDTH), BF16)
     dma = pltpu.SemaphoreType.DMA
     rows = responses.shape[0] * 2
     out = pl.pallas_call(
         functools.partial(kernel, scale),
         out_shape=jax.ShapeDtypeStruct((1, PATCHES), F32),
-        in_specs=[vmem, vmem, smem, smem, smem, vmem, pl.BlockSpec(memory_space=pl.ANY)],
+        in_specs=[pl.BlockSpec(memory_space=pltpu.HBM)] * 7,
         out_specs=vmem,
         scratch_shapes=[
+            pltpu.VMEM((rows, WIDTH), BF16),
+            pltpu.VMEM((rows, WIDTH), BF16),
+            pltpu.SMEM((SLOTS, PATCHES), jnp.int32),
+            pltpu.SMEM((PATCHES,), jnp.int32),
+            pltpu.SMEM((PATCHES,), jnp.int32),
+            pltpu.VMEM((1, PATCHES), jnp.int32),
+            dma((7,)),
             pltpu.VMEM((PLANE, PIECE, WIDTH), BF16),
             quarter,
             quarter,
@@ -371,9 +418,8 @@
             pltpu.VMEM((COLUMN - 1, 1, WIDTH), F32),
             pltpu.VMEM((1, WIDTH), F32),
             pltpu.VMEM((PLANE - 1, 1, WIDTH), F32),
-            dma,
-            dma((PLANE - 1,)),
-            dma,
+            dma((2 * REACH + 1,)),
+            dma((2 * REACH + 1,)),
             dma((2, len(EDGES), 2)),
             dma((2, len(EDGES), 2)),
             dma((2,)),

time: 67.3 us -> 62.9 us (0.935)
  Pallas kernels: 65.9 us -> 61.6 us
    pallas_call x1, Pallas kernels: 65.9 us -> 61.6 us  [body(): pl.pallas_call(functools.partial(kernel, scale), out_shape=jax.ShapeDtype...]
where the time goes in v3:
time: 62.9 us; the launch traced here: 62.8 us
  Pallas kernels  61.6 us (98%)
  local copies, waits for them, and re-layouts  1.19 us (2%)
    pallas_call x1, Pallas kernels, body(): pl.pallas_call(functools.partial(kernel, scale), out_shape=jax.ShapeDtype...  61.6 us

profile of v3, /device:TPU:1, one launch (start us, length us, event | category | flops | bytes accessed | tf_op | source)
XLA Modules:
  0.0 62.8 jit_solution(6369741926930319904)
XLA Ops:
  0.0 61.6 %shard_map.73 = f32[1,96]{1,0:T(1,128)} custom-call(bf16[128,128]{1,0:T(8,128)(2,1)} %bitcast.5, bf16[128,128]{1,0:T(8,128)(2,1)} %bitcast.6, s32[4,96]{1,0:T(4,128)} %bitcast.7, s32[96]{0:T(128)} %counts_hbm.1, s32[96]{0:T(128)} %sizes_hbm.1, s32[1,96]{1,0:T(1,128)} %bitcast.8, bf16[96,4,48,128]{3,2,1,0:T(8,128)(2,1)} %shapes_hbm.1), custom_call_target="tpu_custom_call" | custom-call | flops 2415919104 | bytes 5000000 | tf_op jit(solution)/shard_map/pallas_call | solution.py:394
  61.6 1.2 %copy.9 = f32[96]{0:T(128)} copy(f32[96]{0:T(128)} %bitcast.9) | data formatting | bytes 768

commit v4 on v3

--- a/solution.py
+++ b/solution.py
@@ -23,7 +23,8 @@
 UNROLL = 16
 
 
-EDGES = ((2, 3), (2, 5), (3, 4), (5, 6), (6, 7), (7, 8))
+EDGES = ((2, 3), (2, 5), (3, 4), (5, 6), (5, 8), (6, 7))
+LAST = 7
 REACH = 2
 FAR = RING // 2
 ARRIVAL = (1, 2, 3, 5, 4, 6, 7)
@@ -192,13 +193,12 @@
             device_id_type=MESH,
         )
 
-    def to_far_pair(side):
-        last = slot_of(FAR, side)
+    def to_far_pair(side, part):
         return pltpu.make_async_remote_copy(
-            src_ref=chunk(0, slot_of(FAR - 1, side), side),
-            dst_ref=chunk(1, last, side),
-            send_sem=far_send.at[side],
-            recv_sem=far_recv.at[side],
+            src_ref=chunk(0, slot_of(LAST - 1, side), part),
+            dst_ref=chunk(1, slot_of(LAST, side), part),
+            send_sem=far_send.at[side, part],
+            recv_sem=far_recv.at[side, part],
             device_id=(q, lax.rem(pair[1] + COLUMN + 2 * (1 - 2 * side), COLUMN)),
             device_id_type=MESH,
         )
@@ -220,8 +220,8 @@
         for edge, (near, far) in enumerate(EDGES):
             if near == distance and taken(side, edge, part):
                 along(side, edge, part).start()
-                if far == FAR:
-                    to_far_pair(side).start()
+                if far == LAST:
+                    to_far_pair(side, part).start()
 
     sample = lax.broadcasted_iota(jnp.int32, (SAMPLES, WIDTH), 0)
 
@@ -243,7 +243,7 @@
         if half == 0:
             acc[index] = part
         else:
-            folded[index] = jnp.sum(acc[index] + part, axis=0, keepdims=True)
+            folded[pl.ds(index, 1)] = jnp.sum(acc[index] + part, axis=0, keepdims=True)
 
     def work(half, share, shares):
         length = 2 * UNROLL if shares == 1 else UNROLL
@@ -256,10 +256,12 @@
 
         lax.fori_loop(share * turns, (share + 1) * turns, turn, 0)
 
+    direct = (slot_of(LAST, 0), slot_of(LAST, 1))
+
     def pair_wait(slot):
-        if slot == 2 * FAR - 1:
-            for side in range(2):
-                to_far_pair(side).wait_recv()
+        if slot in direct:
+            for part in range(2):
+                to_far_pair(direct.index(slot), part).wait_recv()
         else:
             to_pair(slot).wait_recv()
 
@@ -288,28 +290,26 @@
     tasks = {
         1: [lambda: turn_over(0)],
         2: [lambda: turn_over(1), lambda: work(0, 0, 6)],
-        3: [lambda: work(0, 1, 6), lambda: work(0, 2, 6)],
-        4: [lambda: work(0, 3, 6), lambda: turn_over(2), lambda: work(0, 4, 6), lambda: work(0, 5, 6)],
+        3: [lambda: work(0, 1, 6), lambda: work(0, 2, 6), lambda: work(0, 3, 6)],
+        4: [lambda: work(0, 4, 6), lambda: work(0, 5, 6), lambda: turn_over(2)],
     }
     for edge, (_, far) in enumerate(EDGES):
-        pending = list(tasks.get(edge, ()))
         for part in range(2):
             for side in range(2):
                 if taken(side, edge, part):
                     along(side, edge, part).wait_recv()
-                    if far < FAR:
-                        send_on(side, far, part)
-                        if part == 1:
-                            to_pair(slot_of(far, side)).start()
-            if part == 0 and len(pending) > 1 and edge > 2:
-                pending.pop(0)()
-        for task in pending:
+                    send_on(side, far, part)
+                    if part == 1 and far not in (LAST, FAR):
+                        to_pair(slot_of(far, side)).start()
+        if far == FAR:
+            to_pair(slot_of(FAR, 0)).start()
+        for task in tasks.get(edge, ()):
             task()
     turn_over(3)
     work(1, 0, 1)
 
     lanes = lax.broadcasted_iota(jnp.int32, (PATCHES, WIDTH), 1)
-    terms = jnp.where(lanes // 8 % 2 == 0, folded[...].reshape(PATCHES, WIDTH), 0.0)
+    terms = jnp.where(lanes // 8 % 2 == 0, folded[...], 0.0)
     terms = jnp.sum(terms, axis=1, keepdims=True) * scale
     spread = terms * to_lane
     high = spread.astype(BF16)
@@ -376,10 +376,12 @@
             for side in range(2):
                 if taken(side, edge, part):
                     along(side, edge, part).wait_send()
-    for side in range(2):
-        to_far_pair(side).wait_send()
-    for slot in range(2 * FAR - 1):
-        to_pair(slot).wait_send()
+    for slot in range(2 * FAR):
+        if slot in direct:
+            for part in range(2):
+                to_far_pair(direct.index(slot), part).wait_send()
+        else:
+            to_pair(slot).wait_send()
     lax.fori_loop(1, COLUMN, column_sent, 0)
     lax.fori_loop(1, PLANE, plane_sent, 0)
 
@@ -413,7 +415,7 @@
             pltpu.VMEM((PLANE + 1, WIDTH, 2 * WIDTH), BF16),
             pltpu.VMEM(patch_shapes.shape, BF16),
             pltpu.VMEM((PATCHES, 8, WIDTH), F32),
-            pltpu.VMEM((PATCHES, 1, WIDTH), F32),
+            pltpu.VMEM((PATCHES, WIDTH), F32),
             pltpu.VMEM((COLUMN, 1, WIDTH), F32),
             pltpu.VMEM((COLUMN - 1, 1, WIDTH), F32),
             pltpu.VMEM((1, WIDTH), F32),
@@ -422,10 +424,10 @@
             dma((2 * REACH + 1,)),
             dma((2, len(EDGES), 2)),
             dma((2, len(EDGES), 2)),
-            dma((2,)),
-            dma((2,)),
-            dma((2 * FAR - 1,)),
-            dma((2 * FAR - 1,)),
+            dma((2, 2)),
+            dma((2, 2)),
+            dma((2 * FAR,)),
+            dma((2 * FAR,)),
             dma((COLUMN - 1,)),
             dma,
             dma((PLANE - 1,)),

time: 62.9 us -> 61.6 us (0.979)
  Pallas kernels: 61.6 us -> 60.3 us
    pallas_call x1, Pallas kernels: 61.6 us -> 60.3 us  [body(): pl.pallas_call(functools.partial(kernel, scale), out_shape=jax.ShapeDtype...]
where the time goes in v4:
time: 61.6 us; the launch traced here: 61.5 us
  Pallas kernels  60.3 us (98%)
  local copies, waits for them, and re-layouts  1.19 us (2%)
    pallas_call x1, Pallas kernels, body(): pl.pallas_call(functools.partial(kernel, scale), out_shape=jax.ShapeDtype...  60.3 us

profile of v4, /device:TPU:1, one launch (start us, length us, event | category | flops | bytes accessed | tf_op | source)
XLA Modules:
  0.0 61.5 jit_solution(7285693889012198903)
XLA Ops:
  0.0 60.3 %shard_map.73 = f32[1,96]{1,0:T(1,128)} custom-call(bf16[128,128]{1,0:T(8,128)(2,1)} %bitcast.5, bf16[128,128]{1,0:T(8,128)(2,1)} %bitcast.6, s32[4,96]{1,0:T(4,128)} %bitcast.7, s32[96]{0:T(128)} %counts_hbm.1, s32[96]{0:T(128)} %sizes_hbm.1, s32[1,96]{1,0:T(1,128)} %bitcast.8, bf16[96,4,48,128]{3,2,1,0:T(8,128)(2,1)} %shapes_hbm.1), custom_call_target="tpu_custom_call" | custom-call | flops 2415919104 | bytes 5000000 | tf_op jit(solution)/shard_map/pallas_call | solution.py:396
  60.3 1.2 %copy.9 = f32[96]{0:T(128)} copy(f32[96]{0:T(128)} %bitcast.9) | data formatting | bytes 768

commit v5 on v4

--- a/solution.py
+++ b/solution.py
@@ -149,7 +149,7 @@
     for at, dz in enumerate(planes):
 
         def mix_start(d, carry, at=at, dz=dz):
-            there = lax.rem(q + d, PLANE)
+            there = lax.rem(q + d + PLANE // 2, PLANE) if dz else lax.rem(q + d, PLANE)
             slot = arrives(dz)
             pltpu.make_async_remote_copy(
                 src_ref=staged.at[there],
@@ -288,7 +288,7 @@
         copy.wait()
 
     tasks = {
-        1: [lambda: turn_over(0)],
+        0: [lambda: turn_over(0)],
         2: [lambda: turn_over(1), lambda: work(0, 0, 6)],
         3: [lambda: work(0, 1, 6), lambda: work(0, 2, 6), lambda: work(0, 3, 6)],
         4: [lambda: work(0, 4, 6), lambda: work(0, 5, 6), lambda: turn_over(2)],

time: 61.6 us -> 60.7 us (0.985)
  Pallas kernels: 60.3 us -> 59.4 us
    pallas_call x1, Pallas kernels: 60.3 us -> 59.4 us  [body(): pl.pallas_call(functools.partial(kernel, scale), out_shape=jax.ShapeDtype...]
where the time goes in v5:
time: 60.7 us; the launch traced here: 60.6 us
  Pallas kernels  59.4 us (98%)
  local copies, waits for them, and re-layouts  1.19 us (2%)
    pallas_call x1, Pallas kernels, body(): pl.pallas_call(functools.partial(kernel, scale), out_shape=jax.ShapeDtype...  59.4 us

profile of v5, /device:TPU:1, one launch (start us, length us, event | category | flops | bytes accessed | tf_op | source)
XLA Modules:
  0.0 60.6 jit_solution(734882985013635026)
XLA Ops:
  0.0 59.4 %shard_map.73 = f32[1,96]{1,0:T(1,128)} custom-call(bf16[128,128]{1,0:T(8,128)(2,1)} %bitcast.5, bf16[128,128]{1,0:T(8,128)(2,1)} %bitcast.6, s32[4,96]{1,0:T(4,128)} %bitcast.7, s32[96]{0:T(128)} %counts_hbm.1, s32[96]{0:T(128)} %sizes_hbm.1, s32[1,96]{1,0:T(1,128)} %bitcast.8, bf16[96,4,48,128]{3,2,1,0:T(8,128)(2,1)} %shapes_hbm.1), custom_call_target="tpu_custom_call" | custom-call | flops 2415919104 | bytes 5000000 | tf_op jit(solution)/shard_map/pallas_call | solution.py:396
  59.4 1.2 %copy.9 = f32[96]{0:T(128)} copy(f32[96]{0:T(128)} %bitcast.9) | data formatting | bytes 768

commit v6 on v5

--- a/solution.py
+++ b/solution.py
@@ -246,7 +246,7 @@
             folded[pl.ds(index, 1)] = jnp.sum(acc[index] + part, axis=0, keepdims=True)
 
     def work(half, share, shares):
-        length = 2 * UNROLL if shares == 1 else UNROLL
+        length = 3 * UNROLL if shares == 1 else UNROLL
         turns = PATCHES // length // shares
 
         def turn(step, carry):

time: 60.7 us -> 60.5 us (level)
  no operation moved by 1% of the time
where the time goes in v6:
time: 60.5 us; the launch traced here: 60.4 us
  Pallas kernels  59.2 us (98%)
  local copies, waits for them, and re-layouts  1.19 us (2%)
    pallas_call x1, Pallas kernels, body(): pl.pallas_call(functools.partial(kernel, scale), out_shape=jax.ShapeDtype...  59.2 us

profile of v6, /device:TPU:1, one launch (start us, length us, event | category | flops | bytes accessed | tf_op | source)
XLA Modules:
  0.0 60.4 jit_solution(6279955523649859202)
XLA Ops:
  0.0 59.2 %shard_map.73 = f32[1,96]{1,0:T(1,128)} custom-call(bf16[128,128]{1,0:T(8,128)(2,1)} %bitcast.5, bf16[128,128]{1,0:T(8,128)(2,1)} %bitcast.6, s32[4,96]{1,0:T(4,128)} %bitcast.7, s32[96]{0:T(128)} %counts_hbm.1, s32[96]{0:T(128)} %sizes_hbm.1, s32[1,96]{1,0:T(1,128)} %bitcast.8, bf16[96,4,48,128]{3,2,1,0:T(8,128)(2,1)} %shapes_hbm.1), custom_call_target="tpu_custom_call" | custom-call | flops 2415919104 | bytes 5000000 | tf_op jit(solution)/shard_map/pallas_call | solution.py:396
  59.2 1.2 %copy.9 = f32[96]{0:T(128)} copy(f32[96]{0:T(128)} %bitcast.9) | data formatting | bytes 768
